TPU v7x, 32 devices: a whole 2x2x4 slice. The times are simulated.
32 devices in a mesh: parts: 2 (over y), dp: 4 (over z), tp: 4 (over x, core).
Axes of the slice: x: 2, y: 2, z: 4, core: 2. Of those that a mesh axis runs over, the one named last changes fastest.
Arguments:
- kcache: bfloat16 [768, 64, 1024], P(('parts', 'dp'), None, 'tp'), parts along dimension 0, may hold values from -6 to 6
- vcache: bfloat16 [768, 64, 1024], P(('parts', 'dp'), None, 'tp'), parts along dimension 0, may hold values from -6 to 6
- send_pages: int32 [8, 4, 3], P(('parts', 'dp')), parts along dimension 0, may hold values from -1 to 95, as said below
- tables: int32 [32, 16], P(('parts', 'dp')), parts along dimension 0, may hold values from 0 to 107, as said below
- lengths: int32 [32], P(('parts', 'dp')), parts along dimension 0, may hold values from 1 to 1020, as said below
- queries: bfloat16 [32, 4, 8192], P(('parts', 'dp'), None, 'tp'), parts along dimension 0, may hold values from -120 to 120
- new_keys: bfloat16 [32, 4, 1024], P(('parts', 'dp'), None, 'tp'), parts along dimension 0, may hold values from -6 to 6
- new_values: bfloat16 [32, 4, 1024], P(('parts', 'dp'), None, 'tp'), parts along dimension 0, may hold values from -6 to 6
- pre_mix: float32 [64, 64], replicated, may hold values from -1.5 to 1.5
- post_mix: float32 [64, 64], replicated, may hold values from -1.5 to 1.5
Outputs:
- attended: bfloat16 [32, 4, 8192], P(('parts', 'dp'), None, 'tp'), parts along dimension 0
There are 2 independent parts, one for each index of `parts`. A program takes and returns all parts, laid end to end along the dimension named above; an argument that names none is the same for every part. Nothing has to cross between parts.
Inputs may be any that keep to these rules, and one draw needn't show every extreme that they name: `send_pages`: each entry is a page id of the source replica or -1; no replica sends to itself; in every draw some source fills all 3 slots to every other replica and some target receives 3 pages from every other source. `tables`: entries name a replica's own pages (below 96) or extended slots 96 + s * 3 + c whose send_pages[s, r, c] is not -1; a page may be named more than once. `lengths`: some sequence has exactly 1020 cached tokens in every draw.
All inputs are finite; a program needn't handle non-finite values.
Results may differ from a plain program's by a relative error of at most 0.0051.
Values may be sent and summed in bfloat16 or wider, within the bound.
A program may use at most 128 MiB of HBM per device.

v0:
```python
import jax
import jax.numpy as jnp
from jax import lax
from jax.sharding import PartitionSpec as P

HEAD = 128


def insert_new(cache_rows, fresh_rows, offset):
    return lax.dynamic_update_slice(cache_rows, fresh_rows, (offset, jnp.zeros((), jnp.int32)))


def softmax_rows(scores, visible):
    masked = jnp.where(visible, scores, -jnp.inf)
    row_max = jnp.max(masked, axis=-1, keepdims=True)
    raised = jnp.exp(masked - row_max)
    return raised / jnp.sum(raised, axis=-1, keepdims=True)


def on_device(
    kcache, vcache, send_pages, tables, lengths, queries, new_keys, new_values, pre_mix, post_mix
):
    highest = lax.Precision.HIGHEST
    outgoing = send_pages[0]
    present = outgoing >= 0
    safe_ids = jnp.where(present, outgoing, 0)
    keep_mask = present[:, :, None, None]
    out_keys = jnp.where(keep_mask, kcache[safe_ids], jnp.zeros((), kcache.dtype))
    out_values = jnp.where(keep_mask, vcache[safe_ids], jnp.zeros((), vcache.dtype))
    came_keys, came_values = (
        lax.all_to_all(out_keys, "dp", split_axis=0, concat_axis=0, tiled=True),
        lax.all_to_all(out_values, "dp", split_axis=0, concat_axis=0, tiled=True),
    )
    page_len = kcache.shape[1]
    local_width = kcache.shape[2]
    pool_keys = jnp.concatenate([kcache, came_keys.reshape(-1, page_len, local_width)], 0)
    pool_values = jnp.concatenate([vcache, came_values.reshape(-1, page_len, local_width)], 0)
    slot_count, table_len = tables.shape
    key_span = table_len * page_len
    key_rows = pool_keys[tables].reshape(slot_count, key_span, local_width)
    value_rows = pool_values[tables].reshape(slot_count, key_span, local_width)
    key_rows = jax.vmap(insert_new)(key_rows, new_keys, lengths)
    value_rows = jax.vmap(insert_new)(value_rows, new_values, lengths)
    step_count = queries.shape[1]
    local_groups = local_width // HEAD
    local_heads = queries.shape[2] // HEAD
    group_size = local_heads // local_groups
    query_blocks = queries.reshape(slot_count, step_count, local_groups, group_size, HEAD)
    key_blocks = key_rows.reshape(slot_count, key_span, local_groups, HEAD)
    logits = jnp.einsum(
        "stgrd,sjgd->stgrj", query_blocks, key_blocks, preferred_element_type=jnp.float32
    ) * HEAD ** (-0.5)
    logits = logits.reshape(slot_count, step_count, local_heads, key_span)
    first_head = lax.axis_index("tp") * local_heads
    step_limit = lengths[:, None, None] + jnp.arange(step_count, dtype=jnp.int32)[None, :, None]
    value_blocks = value_rows.reshape(slot_count, key_span, local_groups, HEAD)
    pre_rows = lax.dynamic_slice_in_dim(pre_mix, first_head, local_heads, 0)
    position = jnp.arange(key_span, dtype=jnp.int32)
    visible = position[None, None, :] <= step_limit
    visible = visible[None]
    columns = pre_rows
    mixed_scores = lax.psum_scatter(
        jnp.einsum("hk,sthj->kstj", columns, logits, precision=highest),
        "tp",
        scatter_dimension=0,
        tiled=True,
    )
    weights = softmax_rows(mixed_scores, visible)
    post_rows = lax.dynamic_slice_in_dim(post_mix, first_head, local_heads, 0)
    columns = post_rows
    blended = lax.psum_scatter(
        jnp.einsum("hk,hstj->kstj", columns, weights, precision=highest),
        "tp",
        scatter_dimension=0,
        tiled=True,
    )
    blended = blended.astype(jnp.bfloat16).reshape(
        local_groups, group_size, slot_count, step_count, key_span
    )
    outputs = jnp.einsum(
        "grstj,sjgd->stgrd", blended, value_blocks, preferred_element_type=jnp.float32
    )
    return outputs.reshape(slot_count, step_count, local_heads * HEAD).astype(jnp.bfloat16)


def solution(mesh):
    in_specs = (
        P(("parts", "dp"), None, "tp"),
        P(("parts", "dp"), None, "tp"),
        P(("parts", "dp"), None, None),
        P(("parts", "dp"), None),
        P(("parts", "dp")),
        P(("parts", "dp"), None, "tp"),
        P(("parts", "dp"), None, "tp"),
        P(("parts", "dp"), None, "tp"),
        P(),
        P(),
    )
    out_specs = P(("parts", "dp"), None, "tp")
    return jax.shard_map(
        on_device, mesh=mesh, in_specs=in_specs, out_specs=out_specs, check_vma=False
    )
```

profile of v0, /device:TPU:0, one launch (start us, length us, event | category | flops | bytes accessed | tf_op | source)
XLA Modules:
  0.0 195.1 jit_solution(2726273615204787622)
XLA Ops:
  6.6 0.8 compare_select_fusion
  7.4 0.9 broadcast_compare_fusion
  8.3 0.1 copy.20
  8.4 0.1 reshape.163
  8.5 3.2 %gather_fusion.2 = bf16[12,64,256]{2,1,0:T(8,128)(2,1)} fusion(bf16[96,64,256]{2,1,0:T(8,128)(2,1)} %param.10, s32[1024]{0:T(1024)S(1)} %pad_clamp_fusion.1), kind=kCustom, calls=%fused_computation.2 | custom fusion | bytes 786480 | tf_op jit(solution)/shard_map/gather | solution.py:28
  11.7 3.2 %gather_fusion = bf16[12,64,256]{2,1,0:T(8,128)(2,1)} fusion(bf16[96,64,256]{2,1,0:T(8,128)(2,1)} %param.11, s32[1024]{0:T(1024)S(1)} %pad_clamp_fusion.1), kind=kCustom, calls=%fused_computation | custom fusion | bytes 786480 | tf_op jit(solution)/shard_map/gather | solution.py:29
  14.9 0.1 copy.19
  15.0 2.2 %broadcast_select_fusion = (bf16[4,3,64,256]{3,2,1,0:T(8,128)(2,1)}, bf16[4,3,64,256]{3,2,1,0:T(8,128)(2,1)}) fusion(bf16[4,3,64,256]{3,2,1,0:T(8,128)(2,1)} %bitcast.72, pred[4,3]{1,0:T(4,128)(4,1)S(1)} %bitcast.74, bf16[4,3,64,256]{3,2,1,0:T(8,128)(2,1)} %bitcast.73), kind=kLoop, calls=%fused_computation.34 | loop fusion | flops 393216 | bytes 1572876 | tf_op jit(solution)/shard_map/jit(_where)/select_n | solution.py:28
  17.2 6.3 %all-to-all-start.1 = ((bf16[4,3,64,256]{3,2,1,0:T(8,128)(2,1)}), bf16[4,3,64,256]{3,2,1,0:T(8,128)(2,1)}, u32[]{:S(2)}, u32[]{:S(2)}) async-start(bf16[4,3,64,256]{3,2,1,0:T(8,128)(2,1)} %get-tuple-element.59), calls=%async_computation.1 | async-start | bytes 786432 | tf_op jit(solution)/shard_map/all_to_all | solution.py:31
  23.5 0.1 reshape.171
  23.6 0.1 pad_clamp_fusion.2
  23.7 0.1 copy.21
  23.9 11.4 %all-to-all-done.1 = bf16[4,3,64,256]{3,2,1,0:T(8,128)(2,1)} async-done(((bf16[4,3,64,256]{3,2,1,0:T(8,128)(2,1)}), bf16[4,3,64,256]{3,2,1,0:T(8,128)(2,1)}, u32[]{:S(2)}, u32[]{:S(2)}) %all-to-all-start.1) | async-done | bytes 393248 | tf_op jit(solution)/shard_map/all_to_all | solution.py:31
  35.3 3.0 %pad_maximum_fusion.1 = bf16[108,64,256]{2,1,0:T(8,128)(2,1)} fusion(bf16[12,64,256]{2,1,0:T(8,128)(2,1)} %bitcast.12, bf16[96,64,256]{2,1,0:T(8,128)(2,1)S(1)} %copy-done.2), kind=kLoop, calls=%fused_computation.11 | loop fusion | flops 1769472 | bytes 7077888 | tf_op jit(solution)/shard_map/concatenate | solution.py:36
  38.3 2.7 %gather_fusion.3 = bf16[64,64,256]{2,1,0:T(8,128)(2,1)S(1)} fusion(bf16[108,64,256]{2,1,0:T(8,128)(2,1)} %pad_maximum_fusion.1, s32[1024]{0:T(1024)S(1)} %pad_clamp_fusion), kind=kCustom, calls=%fused_computation.3 | custom fusion | bytes 4194560 | tf_op jit(solution)/shard_map/gather | solution.py:40
  41.1 29.3 %while.3 = (s32[]{:T(128)}, bf16[4,1024,256]{2,1,0:T(8,128)(2,1)S(1)}, s32[4,3]{1,0:T(4,128)S(1)}, bf16[4,4,256]{2,1,0:T(4,128)(2,1)}, s32[]{:T(128)}, /*index=5*/s32[3]{0:T(128)S(1)}, s32[]{:T(128)}) while((s32[]{:T(128)}, bf16[4,1024,256]{2,1,0:T(8,128)(2,1)S(1)}, s32[4,3]{1,0:T(4,128)S(1)}, bf16[4,4,256]{2,1,0:T(4,128)(2,1)}, s32[]{:T(128)}, ...), condition=%wide.while_cond.1, body=%wide.while_body.1.sunk | while | flops 1043 | bytes 10411 | solution.py:10
  41.1 0.7 fusion.41
  41.7 2.7 %and_reduce_fusion.5 = pred[]{:T(512)} fusion(s32[3]{0:T(128)S(1)} %get-tuple-element.163, s32[1]{0:T(128)} %bitcast.65, s32[1]{0:T(128)} %bitcast.66, s32[1]{0:T(128)} %bitcast.67), kind=kLoop, calls=%fused_computation.8.clone.1 | loop fusion | flops 17 | bytes 25 | tf_op jit(solution)/shard_map/vmap(vmap())/scatter
  44.4 2.6 %dynamic-slice_select_fusion.5 = bf16[1,4,256]{2,1,0:T(4,128)(2,1)S(1)} fusion(bf16[4,4,256]{2,1,0:T(4,128)(2,1)} %get-tuple-element.161, s32[]{:T(128)} %get-tuple-element.151, bf16[4,1024,256]{2,1,0:T(8,128)(2,1)S(1)} %get-tuple-element.152, s32[]{:T(128)} %bitcast.63, s32[]{:T(128)} %bitcast.64, pred[]{:T(512)} %and_reduce_fusion.5), kind=kLoop, calls=%fused_computation.7.clone.1 | loop fusion | flops 1024 | bytes 6157 | tf_op jit(solution)/shard_map/vmap(vmap())/scatter
  47.0 1.4 dynamic-update-slice.7
  48.4 0.7 fusion.41
  49.1 2.7 %and_reduce_fusion.5 = pred[]{:T(512)} fusion(s32[3]{0:T(128)S(1)} %get-tuple-element.163, s32[1]{0:T(128)} %bitcast.65, s32[1]{0:T(128)} %bitcast.66, s32[1]{0:T(128)} %bitcast.67), kind=kLoop, calls=%fused_computation.8.clone.1 | loop fusion | flops 17 | bytes 25 | tf_op jit(solution)/shard_map/vmap(vmap())/scatter
  51.8 2.6 %dynamic-slice_select_fusion.5 = bf16[1,4,256]{2,1,0:T(4,128)(2,1)S(1)} fusion(bf16[4,4,256]{2,1,0:T(4,128)(2,1)} %get-tuple-element.161, s32[]{:T(128)} %get-tuple-element.151, bf16[4,1024,256]{2,1,0:T(8,128)(2,1)S(1)} %get-tuple-element.152, s32[]{:T(128)} %bitcast.63, s32[]{:T(128)} %bitcast.64, pred[]{:T(512)} %and_reduce_fusion.5), kind=kLoop, calls=%fused_computation.7.clone.1 | loop fusion | flops 1024 | bytes 6157 | tf_op jit(solution)/shard_map/vmap(vmap())/scatter
  54.3 1.4 dynamic-update-slice.7
  55.7 0.7 fusion.41
  56.4 2.7 %and_reduce_fusion.5 = pred[]{:T(512)} fusion(s32[3]{0:T(128)S(1)} %get-tuple-element.163, s32[1]{0:T(128)} %bitcast.65, s32[1]{0:T(128)} %bitcast.66, s32[1]{0:T(128)} %bitcast.67), kind=kLoop, calls=%fused_computation.8.clone.1 | loop fusion | flops 17 | bytes 25 | tf_op jit(solution)/shard_map/vmap(vmap())/scatter
  59.1 2.6 %dynamic-slice_select_fusion.5 = bf16[1,4,256]{2,1,0:T(4,128)(2,1)S(1)} fusion(bf16[4,4,256]{2,1,0:T(4,128)(2,1)} %get-tuple-element.161, s32[]{:T(128)} %get-tuple-element.151, bf16[4,1024,256]{2,1,0:T(8,128)(2,1)S(1)} %get-tuple-element.152, s32[]{:T(128)} %bitcast.63, s32[]{:T(128)} %bitcast.64, pred[]{:T(512)} %and_reduce_fusion.5), kind=kLoop, calls=%fused_computation.7.clone.1 | loop fusion | flops 1024 | bytes 6157 | tf_op jit(solution)/shard_map/vmap(vmap())/scatter
  61.7 1.4 dynamic-update-slice.7
  63.1 0.7 fusion.41
  63.7 2.7 %and_reduce_fusion.5 = pred[]{:T(512)} fusion(s32[3]{0:T(128)S(1)} %get-tuple-element.163, s32[1]{0:T(128)} %bitcast.65, s32[1]{0:T(128)} %bitcast.66, s32[1]{0:T(128)} %bitcast.67), kind=kLoop, calls=%fused_computation.8.clone.1 | loop fusion | flops 17 | bytes 25 | tf_op jit(solution)/shard_map/vmap(vmap())/scatter
  66.4 2.6 %dynamic-slice_select_fusion.5 = bf16[1,4,256]{2,1,0:T(4,128)(2,1)S(1)} fusion(bf16[4,4,256]{2,1,0:T(4,128)(2,1)} %get-tuple-element.161, s32[]{:T(128)} %get-tuple-element.151, bf16[4,1024,256]{2,1,0:T(8,128)(2,1)S(1)} %get-tuple-element.152, s32[]{:T(128)} %bitcast.63, s32[]{:T(128)} %bitcast.64, pred[]{:T(512)} %and_reduce_fusion.5), kind=kLoop, calls=%fused_computation.7.clone.1 | loop fusion | flops 1024 | bytes 6157 | tf_op jit(solution)/shard_map/vmap(vmap())/scatter
  69.0 1.4 dynamic-update-slice.7
  70.4 2.1 %reshape.99 = bf16[4,1024,2,128]{3,2,1,0:T(2,128)(2,1)} reshape(bf16[4,1024,256]{2,1,0:T(8,128)(2,1)S(1)} %get-tuple-element.18) | data formatting | bytes 4194304 | tf_op jit(solution)/shard_map/reshape | solution.py:49
  72.5 2.4 %fusion.7 = f32[4,4,2,8,1024]{4,3,1,2,0:T(8,128)S(1)} fusion(bf16[4,1024,2,128,1]{3,2,1,0,4:T(2,128)(2,1)} %bitcast.70, bf16[4,4,2,8,128]{4,3,2,1,0:T(8,128)(2,1)S(1)} %reshape.100), kind=kOutput, calls=%fused_computation.17 | convolution fusion | flops 67371008 | bytes 3211264 | tf_op jit(solution)/shard_map/stgrd,sjgd->stgrj/dot_general | solution.py:50
  74.9 5.0 %fusion.16 = f32[64,4,4,1024]{3,0,2,1:T(8,128)} fusion(f32[4,4,2,8,1024]{4,3,1,2,0:T(8,128)S(1)} %fusion.7, f32[64,64]{1,0:T(8,128)S(1)} %copy-done, s32[]{:T(128)S(6)} %select_n.50), kind=kOutput, calls=%fused_computation.20 | convolution fusion | flops 201326592 | bytes 5251076 | tf_op jit(solution)/shard_map/hk,sthj->kstj/dot_general | solution.py:63
  80.1 0.1 iota_compare_fusion
  80.2 43.5 %reduce-scatter.3.cloned.1.call-done = f32[16,4,4,1024]{3,0,2,1:T(8,128)} async-done(((f32[64,4,4,1024]{3,0,2,1:T(8,128)}), f32[16,4,4,1024]{3,0,2,1:T(8,128)}) %reduce-scatter.3.cloned.1.call-update) | async-done | bytes 1048592 | tf_op jit(solution)/shard_map/reduce_scatter | solution.py:62
  123.7 1.5 select_reduce_fusion
  125.2 1.6 fusion.21
  126.8 5.8 %fusion.19 = f32[64,4,4,1024]{3,0,2,1:T(8,128)} fusion(f32[16,4,4,1024]{3,0,2,1:T(8,128)S(1)} %copy-done.1, f32[16,4,4]{0,2,1:T(4,128)S(1)} %fusion.21, f32[16,4,4]{0,2,1:T(4,128)S(1)} %select_reduce_fusion, pred[4,4,1024]{2,1,0:T(4,128)(4,1)S(1)} %iota_compare_fusion, f32[64,64]{1,0:T(8,128)} %param.19, s32[]{:T(128)S(6)} %select_n.50), kind=kOutput, calls=%fused_computation.23 | convolution fusion | flops 202113024 | bytes 5269508 | tf_op jit(solution)/shard_map/hk,hstj->kstj/dot_general | solution.py:72
  132.6 4.9 %all-to-all-start = ((bf16[4,3,64,256]{3,2,1,0:T(8,128)(2,1)}), bf16[4,3,64,256]{3,2,1,0:T(8,128)(2,1)}, u32[]{:S(2)}, u32[]{:S(2)}) async-start(bf16[4,3,64,256]{3,2,1,0:T(8,128)(2,1)} %get-tuple-element.60), calls=%async_computation | async-start | bytes 786432 | tf_op jit(solution)/shard_map/all_to_all | solution.py:32
  137.5 11.8 %all-to-all-done = bf16[4,3,64,256]{3,2,1,0:T(8,128)(2,1)} async-done(((bf16[4,3,64,256]{3,2,1,0:T(8,128)(2,1)}), bf16[4,3,64,256]{3,2,1,0:T(8,128)(2,1)}, u32[]{:S(2)}, u32[]{:S(2)}) %all-to-all-start) | async-done | bytes 393248 | tf_op jit(solution)/shard_map/all_to_all | solution.py:32
  149.3 3.1 %pad_maximum_fusion = bf16[108,64,256]{2,1,0:T(8,128)(2,1)} fusion(bf16[12,64,256]{2,1,0:T(8,128)(2,1)} %bitcast.3, bf16[96,64,256]{2,1,0:T(8,128)(2,1)S(1)} %copy-done.3), kind=kLoop, calls=%fused_computation.10 | loop fusion | flops 1769472 | bytes 7077888 | tf_op jit(solution)/shard_map/concatenate | solution.py:37
  152.4 2.7 %gather_fusion.1 = bf16[64,64,256]{2,1,0:T(8,128)(2,1)S(1)} fusion(bf16[108,64,256]{2,1,0:T(8,128)(2,1)} %pad_maximum_fusion, s32[1024]{0:T(1024)S(1)} %pad_clamp_fusion), kind=kCustom, calls=%fused_computation.1 | custom fusion | bytes 4194560 | tf_op jit(solution)/shard_map/gather | solution.py:41
  155.1 28.1 %while.2 = (s32[]{:T(128)}, bf16[4,1024,256]{2,1,0:T(8,128)(2,1)S(1)}, s32[4,3]{1,0:T(4,128)S(1)}, bf16[4,4,256]{2,1,0:T(4,128)(2,1)}, s32[]{:T(128)}, /*index=5*/s32[3]{0:T(128)S(1)}, s32[]{:T(128)}) while((s32[]{:T(128)}, bf16[4,1024,256]{2,1,0:T(8,128)(2,1)S(1)}, s32[4,3]{1,0:T(4,128)S(1)}, bf16[4,4,256]{2,1,0:T(4,128)(2,1)}, s32[]{:T(128)}, ...), condition=%wide.while_cond, body=%wide.while_body.sunk | while | flops 1043 | bytes 10411 | solution.py:10
  155.1 0.6 fusion.40
  155.7 2.5 %and_reduce_fusion.4 = pred[]{:T(512)} fusion(s32[3]{0:T(128)S(1)} %get-tuple-element.142, s32[1]{0:T(128)} %bitcast.60, s32[1]{0:T(128)} %bitcast.61, s32[1]{0:T(128)} %bitcast.62), kind=kLoop, calls=%fused_computation.5.clone.1 | loop fusion | flops 17 | bytes 25 | tf_op jit(solution)/shard_map/vmap(vmap())/scatter
  158.3 2.5 %dynamic-slice_select_fusion.4 = bf16[1,4,256]{2,1,0:T(4,128)(2,1)S(1)} fusion(bf16[4,4,256]{2,1,0:T(4,128)(2,1)} %get-tuple-element.140, s32[]{:T(128)} %get-tuple-element.130, bf16[4,1024,256]{2,1,0:T(8,128)(2,1)S(1)} %get-tuple-element.131, s32[]{:T(128)} %bitcast.58, s32[]{:T(128)} %bitcast.59, pred[]{:T(512)} %and_reduce_fusion.4), kind=kLoop, calls=%fused_computation.4.clone.1 | loop fusion | flops 1024 | bytes 6157 | tf_op jit(solution)/shard_map/vmap(vmap())/scatter
  160.8 1.4 dynamic-update-slice.6
  162.1 0.6 fusion.40
  162.8 2.5 %and_reduce_fusion.4 = pred[]{:T(512)} fusion(s32[3]{0:T(128)S(1)} %get-tuple-element.142, s32[1]{0:T(128)} %bitcast.60, s32[1]{0:T(128)} %bitcast.61, s32[1]{0:T(128)} %bitcast.62), kind=kLoop, calls=%fused_computation.5.clone.1 | loop fusion | flops 17 | bytes 25 | tf_op jit(solution)/shard_map/vmap(vmap())/scatter
  165.3 2.5 %dynamic-slice_select_fusion.4 = bf16[1,4,256]{2,1,0:T(4,128)(2,1)S(1)} fusion(bf16[4,4,256]{2,1,0:T(4,128)(2,1)} %get-tuple-element.140, s32[]{:T(128)} %get-tuple-element.130, bf16[4,1024,256]{2,1,0:T(8,128)(2,1)S(1)} %get-tuple-element.131, s32[]{:T(128)} %bitcast.58, s32[]{:T(128)} %bitcast.59, pred[]{:T(512)} %and_reduce_fusion.4), kind=kLoop, calls=%fused_computation.4.clone.1 | loop fusion | flops 1024 | bytes 6157 | tf_op jit(solution)/shard_map/vmap(vmap())/scatter
  167.8 1.4 dynamic-update-slice.6
  169.2 0.6 fusion.40
  169.8 2.5 %and_reduce_fusion.4 = pred[]{:T(512)} fusion(s32[3]{0:T(128)S(1)} %get-tuple-element.142, s32[1]{0:T(128)} %bitcast.60, s32[1]{0:T(128)} %bitcast.61, s32[1]{0:T(128)} %bitcast.62), kind=kLoop, calls=%fused_computation.5.clone.1 | loop fusion | flops 17 | bytes 25 | tf_op jit(solution)/shard_map/vmap(vmap())/scatter
  172.3 2.5 %dynamic-slice_select_fusion.4 = bf16[1,4,256]{2,1,0:T(4,128)(2,1)S(1)} fusion(bf16[4,4,256]{2,1,0:T(4,128)(2,1)} %get-tuple-element.140, s32[]{:T(128)} %get-tuple-element.130, bf16[4,1024,256]{2,1,0:T(8,128)(2,1)S(1)} %get-tuple-element.131, s32[]{:T(128)} %bitcast.58, s32[]{:T(128)} %bitcast.59, pred[]{:T(512)} %and_reduce_fusion.4), kind=kLoop, calls=%fused_computation.4.clone.1 | loop fusion | flops 1024 | bytes 6157 | tf_op jit(solution)/shard_map/vmap(vmap())/scatter
  174.8 1.4 dynamic-update-slice.6
  176.2 0.6 fusion.40
  176.8 2.5 %and_reduce_fusion.4 = pred[]{:T(512)} fusion(s32[3]{0:T(128)S(1)} %get-tuple-element.142, s32[1]{0:T(128)} %bitcast.60, s32[1]{0:T(128)} %bitcast.61, s32[1]{0:T(128)} %bitcast.62), kind=kLoop, calls=%fused_computation.5.clone.1 | loop fusion | flops 17 | bytes 25 | tf_op jit(solution)/shard_map/vmap(vmap())/scatter
  179.4 2.5 %dynamic-slice_select_fusion.4 = bf16[1,4,256]{2,1,0:T(4,128)(2,1)S(1)} fusion(bf16[4,4,256]{2,1,0:T(4,128)(2,1)} %get-tuple-element.140, s32[]{:T(128)} %get-tuple-element.130, bf16[4,1024,256]{2,1,0:T(8,128)(2,1)S(1)} %get-tuple-element.131, s32[]{:T(128)} %bitcast.58, s32[]{:T(128)} %bitcast.59, pred[]{:T(512)} %and_reduce_fusion.4), kind=kLoop, calls=%fused_computation.4.clone.1 | loop fusion | flops 1024 | bytes 6157 | tf_op jit(solution)/shard_map/vmap(vmap())/scatter
  181.8 1.4 dynamic-update-slice.6
  183.2 2.1 %reshape.96 = bf16[4,1024,2,128]{3,2,1,0:T(2,128)(2,1)} reshape(bf16[4,1024,256]{2,1,0:T(8,128)(2,1)S(1)} %get-tuple-element.10) | data formatting | bytes 4194304 | tf_op jit(solution)/shard_map/reshape | solution.py:56
  185.3 2.3 %fusion.13 = bf16[4,4,2,8,128]{4,3,1,2,0:T(8,128)(2,1)S(1)} fusion(bf16[4,1024,2,128,1]{3,2,1,0,4:T(2,128)(2,1)} %bitcast.71, f32[16,4,4,1024]{3,0,2,1:T(8,128)} %reduce-scatter.5.cloned.1.call-done), kind=kOutput, calls=%fused_computation.19 | convolution fusion | flops 67403776 | bytes 3211264 | tf_op jit(solution)/shard_map/grstj,sjgd->stgrd/dot_general | solution.py:80
  187.6 0.6 convert_element_type.15
  (40 shorter events, 0.3 us)
Async XLA Ops:
  6.5 68.4 %copy-start = (f32[64,64]{1,0:T(8,128)S(1)}, f32[64,64]{1,0:T(8,128)}, u32[]{:S(2)}) copy-start(f32[64,64]{1,0:T(8,128)} %param.18) | copy-start | bytes 49156
  6.5 17.1 %copy-start.8 = (s32[2]{0:T(128)S(1)}, s32[2]{0:T(128)}, u32[]{:S(2)}) copy-start(s32[2]{0:T(128)} %constant.17.clone.1) | copy-start | bytes 28
  6.5 28.8 %copy-start.2 = (bf16[96,64,256]{2,1,0:T(8,128)(2,1)S(1)}, bf16[96,64,256]{2,1,0:T(8,128)(2,1)}, u32[]{:S(2)}) copy-start(bf16[96,64,256]{2,1,0:T(8,128)(2,1)} %param.10) | copy-start | bytes 9437188
  6.5 17.0 %copy-start.6 = (s32[4,16]{1,0:T(4,128)S(1)}, s32[4,16]{1,0:T(4,128)}, u32[]{:S(2)}) copy-start(s32[4,16]{1,0:T(4,128)} %param.13) | copy-start | bytes 772
  6.5 17.1 %copy-start.7 = (s32[4]{0:T(128)S(1)}, s32[4]{0:T(128)}, u32[]{:S(2)}) copy-start(s32[4]{0:T(128)} %param.14) | copy-start | bytes 52
  6.5 17.2 %copy-start.4 = (bf16[4,4,2048]{2,1,0:T(4,128)(2,1)S(1)}, bf16[4,4,2048]{2,1,0:T(4,128)(2,1)}, u32[]{:S(2)}) copy-start(bf16[4,4,2048]{2,1,0:T(4,128)(2,1)} %param.15) | copy-start | bytes 196612
  17.2 18.1 %all-to-all-start.1 = ((bf16[4,3,64,256]{3,2,1,0:T(8,128)(2,1)}), bf16[4,3,64,256]{3,2,1,0:T(8,128)(2,1)}, u32[]{:S(2)}, u32[]{:S(2)}) async-start(bf16[4,3,64,256]{3,2,1,0:T(8,128)(2,1)} %get-tuple-element.59), calls=%async_computation.1 | async-start | bytes 786432 | tf_op jit(solution)/shard_map/all_to_all | solution.py:31
  23.5 100.2 %reduce-scatter.3.cloned.1.call-start = ((), (), s32[]{:S(2)}) async-start(), calls=%async_computation.4 | async-start | bytes 5242880 | tf_op jit(solution)/shard_map/reduce_scatter | solution.py:62
  38.3 2.7 %copy-start.5 = (s32[3]{0:T(128)S(1)}, s32[3]{0:T(128)}, u32[]{:S(2)}) copy-start(s32[3]{0:T(128)} %constant.127) | copy-start | bytes 40
  80.0 105.3 %reduce-scatter.5.cloned.1.call-start = ((), (), s32[]{:S(2)}) async-start(), calls=%async_computation.5 | async-start | bytes 5242880 | tf_op jit(solution)/shard_map/reduce_scatter | solution.py:71
  123.7 3.1 %copy-start.1 = (f32[16,4,4,1024]{3,0,2,1:T(8,128)S(1)}, f32[16,4,4,1024]{3,0,2,1:T(8,128)}, u32[]{:S(2)}) copy-start(f32[16,4,4,1024]{3,0,2,1:T(8,128)} %reduce-scatter.3.cloned.1.call-done) | copy-start | bytes 3145732
  132.6 16.7 %copy-start.3 = (bf16[96,64,256]{2,1,0:T(8,128)(2,1)S(1)}, bf16[96,64,256]{2,1,0:T(8,128)(2,1)}, u32[]{:S(2)}) copy-start(bf16[96,64,256]{2,1,0:T(8,128)(2,1)} %param.11) | copy-start | bytes 9437188
  132.6 16.7 %all-to-all-start = ((bf16[4,3,64,256]{3,2,1,0:T(8,128)(2,1)}), bf16[4,3,64,256]{3,2,1,0:T(8,128)(2,1)}, u32[]{:S(2)}, u32[]{:S(2)}) async-start(bf16[4,3,64,256]{3,2,1,0:T(8,128)(2,1)} %get-tuple-element.60), calls=%async_computation | async-start | bytes 786432 | tf_op jit(solution)/shard_map/all_to_all | solution.py:32
Sparse Core Ops, SparseCore 0:
  80.1 43.5 reduce-scatter.2
  132.8 44.5 reduce-scatter.4
where the time goes:
time: 196 us; the launch traced here: 195 us
  waiting for transfers between devices  66.8 us (34%)
  other arithmetic  54.4 us (28%)
  local copies, waits for them, and re-layouts  33.3 us (17%)
  matrix products  15.5 us (8%)
  between operations  13.5 us (7%)
  starting transfers between devices  11.2 us (6%)
    reduce_scatter x1, waiting for transfers between devices, on_device(): lax.psum_scatter(jnp.einsum('hk,sthj->kstj', columns, logits, precision=h...  43.5 us
    scatter x16, other arithmetic  41 us
    scatter x24, local copies, waits for them, and re-layouts  16.1 us
    all_to_all x1, waiting for transfers between devices, on_device(): lax.all_to_all(out_values, 'dp', split_axis=0, concat_axis=0, tiled=True)  11.8 us
    all_to_all x1, waiting for transfers between devices, on_device(): lax.all_to_all(out_keys, 'dp', split_axis=0, concat_axis=0, tiled=True)  11.4 us
    all_to_all x1, starting transfers between devices, on_device(): lax.all_to_all(out_keys, 'dp', split_axis=0, concat_axis=0, tiled=True)  6.32 us
    dot_general x1, matrix products, on_device(): jnp.einsum('hk,hstj->kstj', columns, weights, precision=highest)  5.78 us
    dot_general x1, matrix products, on_device(): jnp.einsum('hk,sthj->kstj', columns, logits, precision=highest)  5.05 us
  transfers between devices with their start and end apart: 4, of which 3 were waited for; matrix products, arithmetic and copies ran while one was open for 19% of the time, Pallas kernels for 0%

commit v1 on v0

v1 whole, which is shorter than its diff:
```python
import functools

import jax
import jax.numpy as jnp
from jax import lax
from jax.experimental import pallas as pl
from jax.experimental.pallas import tpu as pltpu
from jax.sharding import PartitionSpec as P

HEAD = 128
MESH = pl.DeviceIdType.MESH
HIGHEST = lax.Precision.HIGHEST


def each(count, body):
    if count <= 4:
        for step in range(count):
            body(step)
    else:

        def looped(step, carry):
            body(step)
            return carry

        lax.fori_loop(0, count, looped, 0)


def kernel(
    n_dp,
    n_tp,
    send_ref,
    tables_ref,
    lengths_ref,
    kcache_ref,
    vcache_ref,
    queries_ref,
    newk_ref,
    newv_ref,
    pre_ref,
    post_ref,
    out_ref,
    ext_k,
    ext_v,
    stage_k,
    stage_v,
    in_k,
    in_v,
    q_wide,
    key_rows,
    value_rows,
    raw_send,
    raw_all,
    mix_t,
    blend_send,
    blend_in,
    res,
    load_sem,
    ks_sem,
    kr_sem,
    vs_sem,
    vr_sem,
    rs_sem,
    rr_sem,
    bs_sem,
    br_sem,
):
    pages, page_len, width = kcache_ref.shape
    cap = send_ref.shape[2]
    slots, maxp = tables_ref.shape
    steps = queries_ref.shape[1]
    heads = queries_ref.shape[2] // HEAD
    groups = width // HEAD
    group_size = heads // groups
    span = maxp * page_len
    dp = lax.axis_index("dp")
    tp = lax.axis_index("tp")

    barrier = pltpu.get_barrier_semaphore()
    for o in range(1, n_dp):
        pl.semaphore_signal(
            barrier, inc=1, device_id={"dp": lax.rem(dp + o, n_dp)}, device_id_type=MESH
        )
    for o in range(1, n_tp):
        pl.semaphore_signal(
            barrier, inc=1, device_id={"tp": lax.rem(tp + o, n_tp)}, device_id_type=MESH
        )

    parts = load_sem.shape[1]
    chunk = pages // parts

    def load(which, cache, ext, part):
        rows = pl.ds(part * chunk, chunk)
        return pltpu.make_async_copy(cache.at[rows], ext.at[rows], load_sem.at[which, part])

    for part in range(parts):
        load(0, kcache_ref, ext_k, part).start()
    for part in range(parts):
        load(1, vcache_ref, ext_v, part).start()

    def page_copy(stage, inbox, s_sem, r_sem, o):
        return pltpu.make_async_remote_copy(
            src_ref=stage.at[pl.ds(o * cap, cap)],
            dst_ref=inbox.at[pl.ds(dp * cap, cap)],
            send_sem=s_sem.at[o],
            recv_sem=r_sem.at[o],
            device_id={"dp": lax.rem(dp + o + 1, n_dp)},
            device_id_type=MESH,
        )

    def stage_pages(stage, ext, o):
        target = lax.rem(dp + o + 1, n_dp)
        for c in range(cap):
            page = jnp.maximum(send_ref[0, target, c], 0)
            stage[o * cap + c] = ext[page]

    pl.semaphore_wait(barrier, n_dp + n_tp - 2)
    for part in range(parts):
        load(0, kcache_ref, ext_k, part).wait()

    def send_k(o):
        stage_pages(stage_k, ext_k, o)
        page_copy(stage_k, in_k, ks_sem, kr_sem, o).start()

    each(n_dp - 1, send_k)

    q_wide[...] = jnp.zeros_like(q_wide)
    for s in range(slots):
        for h in range(heads):
            g = h // group_size
            q_wide[s, g, pl.ds(h, steps, stride=heads), :] = queries_ref[
                s, :, h * HEAD : (h + 1) * HEAD
            ].astype(jnp.float32)
    mix_t[0] = pre_ref[...].T
    mix_t[1] = post_ref[...].T

    for part in range(parts):
        load(1, vcache_ref, ext_v, part).wait()
    each(n_dp - 1, lambda o: stage_pages(stage_v, ext_v, o))

    def take_in(inbox, ext, copy):
        def body(o):
            copy(o).wait_recv()
            source = lax.rem(dp + n_dp - 1 - o, n_dp)
            for c in range(cap):
                ext[pages + source * cap + c] = inbox[source * cap + c]

        each(n_dp - 1, body)

    take_in(in_k, ext_k, lambda o: page_copy(stage_k, in_k, ks_sem, kr_sem, o))
    each(n_dp - 1, lambda o: page_copy(stage_v, in_v, vs_sem, vr_sem, o).start())

    position = lax.broadcasted_iota(jnp.int32, (steps * heads, span), 1)

    def raw_of(s):
        for p in range(maxp):
            key_rows[pl.ds(p * page_len, page_len), :] = ext_k[tables_ref[s, p]]
        rows = jnp.concatenate([q_wide[s, g] for g in range(groups)], axis=1).astype(
            jnp.bfloat16
        )
        contract = (((1,), (1,)), ((), ()))
        raw = lax.dot_general(
            rows, key_rows[...], contract, preferred_element_type=jnp.float32
        )
        fresh = lax.dot_general(
            rows, newk_ref[s], contract, preferred_element_type=jnp.float32
        )
        first = lengths_ref[s]
        for t in range(steps):
            raw = jnp.where(position == first + t, fresh[:, t : t + 1], raw)
        return raw * (HEAD ** (-0.5))

    def raw_copy(o, t):
        return pltpu.make_async_remote_copy(
            src_ref=raw_send.at[o - 1, t],
            dst_ref=raw_all.at[t, pl.ds(tp * heads, heads)],
            send_sem=rs_sem.at[o - 1, t],
            recv_sem=rr_sem.at[o - 1, t],
            device_id={"tp": lax.rem(tp + o, n_tp)},
            device_id_type=MESH,
        )

    half = n_tp // 2
    order = [half] + [o for o in range(1, n_tp) if o != half]
    early = steps // 2
    for o in order:
        raw = raw_of(lax.rem(tp + o, n_tp))
        for t in range(steps):
            raw_send[o - 1, t] = raw[t * heads : (t + 1) * heads]
        for t in range(early):
            raw_copy(o, t).start()
    for t in range(early, steps):
        for o in order:
            raw_copy(o, t).start()
    raw = raw_of(tp)
    for t in range(steps):
        raw_all[t, pl.ds(tp * heads, heads), :] = raw[t * heads : (t + 1) * heads]

    def blend_copy(o, t):
        peer = lax.rem(tp + o, n_tp)
        return pltpu.make_async_remote_copy(
            src_ref=blend_send.at[t, pl.ds(peer * heads, heads)],
            dst_ref=blend_in.at[tp, pl.ds(t * heads, heads)],
            send_sem=bs_sem.at[o - 1, t],
            recv_sem=br_sem.at[o - 1, t],
            device_id={"tp": peer},
            device_id_type=MESH,
        )

    spot = lax.broadcasted_iota(jnp.int32, (n_tp * heads, span), 1)
    own_length = lengths_ref[tp]

    def mix(t):
        for o in order:
            raw_copy(o, t).wait_recv()
        mixed = jnp.dot(
            mix_t[0], raw_all[t], precision=HIGHEST, preferred_element_type=jnp.float32
        )
        mixed = jnp.where(spot <= own_length + t, mixed, -jnp.inf)
        raised = jnp.exp(mixed - jnp.max(mixed, axis=1, keepdims=True))
        weights = raised / jnp.sum(raised, axis=1, keepdims=True)
        blended = jnp.dot(
            mix_t[1], weights, precision=HIGHEST, preferred_element_type=jnp.float32
        )
        blend_send[t] = blended.astype(jnp.bfloat16)
        for o in order:
            blend_copy(o, t).start()
        blend_in[tp, pl.ds(t * heads, heads), :] = blend_send[t, pl.ds(tp * heads, heads), :]

    row = lax.broadcasted_iota(jnp.int32, (page_len, width), 0)

    def gather_values(s):
        first = lengths_ref[s]
        fresh = newv_ref[s].astype(jnp.float32)
        for p in range(maxp):
            page = ext_v[tables_ref[s, p]].astype(jnp.float32)
            for t in range(steps):
                page = jnp.where(row == first + t - p * page_len, fresh[t : t + 1, :], page)
            value_rows[s, pl.ds(p * page_len, page_len), :] = page.astype(jnp.bfloat16)

    for t in range(steps - 1):
        mix(t)
    take_in(in_v, ext_v, lambda o: page_copy(stage_v, in_v, vs_sem, vr_sem, o))
    for s in range(slots):
        gather_values(s)
    mix(steps - 1)

    for o in [0] + [n_tp - o for o in order]:
        s = lax.rem(tp + o, n_tp)
        if o:
            for t in range(steps):
                blend_copy(n_tp - o, t).wait_recv()
        result = jnp.dot(blend_in[s], value_rows[s], preferred_element_type=jnp.float32)
        for g in range(groups):
            res[g] = result[:, g * HEAD : (g + 1) * HEAD]
        for h in range(heads):
            out_ref[s, :, h * HEAD : (h + 1) * HEAD] = res[
                h // group_size, pl.ds(h, steps, stride=heads), :
            ].astype(out_ref.dtype)

    def all_sent(o):
        page_copy(stage_k, in_k, ks_sem, kr_sem, o).wait_send()
        page_copy(stage_v, in_v, vs_sem, vr_sem, o).wait_send()

    each(n_dp - 1, all_sent)
    for t in range(steps):
        for o in order:
            raw_copy(o, t).wait_send()
            blend_copy(o, t).wait_send()


def on_device(
    n_dp,
    n_tp,
    kcache,
    vcache,
    send_pages,
    tables,
    lengths,
    queries,
    new_keys,
    new_values,
    pre_mix,
    post_mix,
):
    pages, page_len, width = kcache.shape
    cap = send_pages.shape[2]
    slots, maxp = tables.shape
    steps = queries.shape[1]
    heads = queries.shape[2] // HEAD
    groups = width // HEAD
    span = maxp * page_len
    all_heads = heads * n_tp
    load_parts = 4
    vmem = pl.BlockSpec(memory_space=pltpu.VMEM)
    smem = pl.BlockSpec(memory_space=pltpu.SMEM)
    hbm = pl.BlockSpec(memory_space=pl.ANY)
    moved = (n_dp - 1) * cap
    bf16, f32 = jnp.bfloat16, jnp.float32
    dma = pltpu.SemaphoreType.DMA
    return pl.pallas_call(
        functools.partial(kernel, n_dp, n_tp),
        out_shape=jax.ShapeDtypeStruct(queries.shape, bf16),
        in_specs=[smem, smem, smem, hbm, hbm, vmem, vmem, vmem, vmem, vmem],
        out_specs=vmem,
        scratch_shapes=[
            pltpu.VMEM((pages + n_dp * cap, page_len, width), bf16),
            pltpu.VMEM((pages + n_dp * cap, page_len, width), bf16),
            pltpu.VMEM((moved, page_len, width), bf16),
            pltpu.VMEM((moved, page_len, width), bf16),
            pltpu.VMEM((n_dp * cap, page_len, width), bf16),
            pltpu.VMEM((n_dp * cap, page_len, width), bf16),
            pltpu.VMEM((slots, groups, steps * heads, HEAD), f32),
            pltpu.VMEM((span, width), bf16),
            pltpu.VMEM((slots, span, width), bf16),
            pltpu.VMEM((n_tp - 1, steps, heads, span), f32),
            pltpu.VMEM((steps, all_heads, span), f32),
            pltpu.VMEM((2, all_heads, all_heads), f32),
            pltpu.VMEM((steps, all_heads, span), bf16),
            pltpu.VMEM((slots, steps * heads, span), bf16),
            pltpu.VMEM((groups, steps * heads, HEAD), f32),
            dma((2, load_parts)),
            dma((n_dp - 1,)),
            dma((n_dp - 1,)),
            dma((n_dp - 1,)),
            dma((n_dp - 1,)),
            dma((n_tp - 1, steps)),
            dma((n_tp - 1, steps)),
            dma((n_tp - 1, steps)),
            dma((n_tp - 1, steps)),
        ],
        compiler_params=pltpu.CompilerParams(
            collective_id=0, has_side_effects=True, vmem_limit_bytes=48 * 1024 * 1024
        ),
    )(
        send_pages,
        tables,
        lengths,
        kcache,
        vcache,
        queries,
        new_keys,
        new_values,
        pre_mix,
        post_mix,
    )


def solution(mesh):
    in_specs = (
        P(("parts", "dp"), None, "tp"),
        P(("parts", "dp"), None, "tp"),
        P(("parts", "dp"), None, None),
        P(("parts", "dp"), None),
        P(("parts", "dp")),
        P(("parts", "dp"), None, "tp"),
        P(("parts", "dp"), None, "tp"),
        P(("parts", "dp"), None, "tp"),
        P(),
        P(),
    )
    out_specs = P(("parts", "dp"), None, "tp")
    return jax.shard_map(
        functools.partial(on_device, mesh.shape["dp"], mesh.shape["tp"]),
        mesh=mesh,
        in_specs=in_specs,
        out_specs=out_specs,
        check_vma=False,
    )
```

time: 196 us -> 42.2 us (0.22)
  waiting for transfers between devices: 66.8 us -> 0 us
  other arithmetic: 54.4 us -> 0 us
  Pallas kernels: 0 us -> 33.3 us
  local copies, waits for them, and re-layouts: 33.3 us -> 8.37 us
  matrix products: 15.5 us -> 0 us
  between operations: 13.5 us -> 0.02 us
  starting transfers between devices: 11.2 us -> 0 us
    reduce_scatter x2 -> x0, waiting for transfers between devices: 43.5 us -> none  [the longest x1 43.5 us: on_device(): lax.psum_scatter(jnp.einsum('hk,sthj->kstj', columns, logits, precision=h...]
    scatter x17 -> x0, other arithmetic: 41.1 us -> none
    pallas_call x0 -> x1, Pallas kernels: none -> 33.3 us  [on_device(): pl.pallas_call(functools.partial(kernel, n_dp, n_tp), out_shape=jax.Shape...]
    all_to_all x2 -> x0, waiting for transfers between devices: 23.2 us -> none  [the longest x1 11.8 us: on_device(): lax.all_to_all(out_values, 'dp', split_axis=0, concat_axis=0, tiled=True)]
    scatter x24 -> x0, local copies, waits for them, and re-layouts: 16.1 us -> none
    dot_general x4 -> x0, matrix products: 15.5 us -> none  [the longest x1 5.78 us: on_device(): jnp.einsum('hk,hstj->kstj', columns, weights, precision=highest)]
    gather x4 -> x0, local copies, waits for them, and re-layouts: 11.8 us -> none  [the longest x1 3.23 us: on_device(): vcache[safe_ids]]
    all_to_all x2 -> x0, starting transfers between devices: 11.2 us -> none  [the longest x1 6.32 us: on_device(): lax.all_to_all(out_keys, 'dp', split_axis=0, concat_axis=0, tiled=True)]
  transfers between devices with their start and end apart: 4 -> 0, of which waited for: 3 -> 0; matrix products, arithmetic and copies ran while one was open for 19% -> 0% of each run, Pallas kernels for 0% -> 0%
where the time goes in v1:
time: 42.2 us; the launch traced here: 41.7 us
  Pallas kernels  33.3 us (79%)
  local copies, waits for them, and re-layouts  8.37 us (20%)
    pallas_call x1, Pallas kernels, on_device(): pl.pallas_call(functools.partial(kernel, n_dp, n_tp), out_shape=jax.Shape...  33.3 us
    unnamed x18, local copies, waits for them, and re-layouts  8.37 us

profile of v1, /device:TPU:0, one launch (start us, length us, event | category | flops | bytes accessed | tf_op | source)
XLA Modules:
  0.0 41.7 jit_solution(2849580918183817146)
XLA Ops:
  0.0 0.8 %copy.11.send_ref = s32[1,4,3]{2,1,0:T(4,128)S(1)} copy(s32[1,4,3]{1,0,2:T(1,128)} %param.12) | data formatting | bytes 96 | tf_op args[2]
  0.8 0.0 copy-start
  0.8 1.9 %copy-done = bf16[96,64,256]{2,1,0:T(8,128)(2,1)S(1)} copy-done((bf16[96,64,256]{2,1,0:T(8,128)(2,1)S(1)}, bf16[96,64,256]{2,1,0:T(8,128)(2,1)}, u32[]{:S(2)}) %copy-start) | copy-done | bytes 3145752
  2.7 0.0 copy-start.1
  2.7 0.8 %copy-done.1 = bf16[4,4,2048]{2,1,0:T(4,128)(2,1)S(1)} copy-done((bf16[4,4,2048]{2,1,0:T(4,128)(2,1)S(1)}, bf16[4,4,2048]{2,1,0:T(4,128)(2,1)}, u32[]{:S(2)}) %copy-start.1) | copy-done | bytes 65560
  3.5 0.0 copy-start.2
  3.5 0.8 %copy-done.2 = f32[64,64]{1,0:T(8,128)S(1)} copy-done((f32[64,64]{1,0:T(8,128)S(1)}, f32[64,64]{1,0:T(8,128)}, u32[]{:S(2)}) %copy-start.2) | copy-done | bytes 16408
  4.3 0.0 copy-start.3
  4.3 0.8 %copy-done.3 = f32[64,64]{1,0:T(8,128)S(1)} copy-done((f32[64,64]{1,0:T(8,128)S(1)}, f32[64,64]{1,0:T(8,128)}, u32[]{:S(2)}) %copy-start.3) | copy-done | bytes 16408
  5.0 0.0 copy-start.4
  5.0 0.7 %copy-done.4 = bf16[4,4,256]{2,1,0:T(4,128)(2,1)S(1)} copy-done((bf16[4,4,256]{2,1,0:T(4,128)(2,1)S(1)}, bf16[4,4,256]{2,1,0:T(4,128)(2,1)}, u32[]{:S(2)}) %copy-start.4) | copy-done | bytes 8216
  5.7 0.0 copy-start.5
  5.7 0.7 %copy-done.5 = bf16[4,4,256]{2,1,0:T(4,128)(2,1)S(1)} copy-done((bf16[4,4,256]{2,1,0:T(4,128)(2,1)S(1)}, bf16[4,4,256]{2,1,0:T(4,128)(2,1)}, u32[]{:S(2)}) %copy-start.5) | copy-done | bytes 8216
  6.4 0.0 copy-start.6
  6.4 0.7 %copy-done.6 = s32[4,16]{1,0:T(4,128)S(1)} copy-done((s32[4,16]{1,0:T(4,128)S(1)}, s32[4,16]{1,0:T(4,128)}, u32[]{:S(2)}) %copy-start.6) | copy-done | bytes 280
  7.1 0.0 copy-start.7
  7.1 0.7 %copy-done.7 = s32[4]{0:T(128)S(1)} copy-done((s32[4]{0:T(128)S(1)}, s32[4]{0:T(128)}, u32[]{:S(2)}) %copy-start.7) | copy-done | bytes 40
  7.7 33.3 %shard_map.100 = bf16[4,4,2048]{2,1,0:T(4,128)(2,1)S(1)} custom-call(s32[1,4,3]{2,1,0:T(4,128)S(1)} %copy.11.send_ref, s32[4,16]{1,0:T(4,128)S(1)} %copy-done.6, s32[4]{0:T(128)S(1)} %copy-done.7, bf16[96,64,256]{2,1,0:T(8,128)(2,1)S(1)} %copy-done, bf16[96,64,256]{2,1,0:T(8,128)(2,1)} %vcache_ref.1, bf16[4,4,2048]{2,1,0:T(4,128)(2,1)S(1)} %copy-done.1, ...), custom_call_target="tpu_custom_call" | custom-call | tf_op jit(solution)/shard_map/pallas_call | solution.py:300
  41.1 0.6 %copy.13 = bf16[4,4,2048]{2,1,0:T(4,128)(2,1)} copy(bf16[4,4,2048]{2,1,0:T(4,128)(2,1)S(1)} %shard_map.100) | data formatting | bytes 131072
Async XLA Ops:
  0.8 1.9 %copy-start = (bf16[96,64,256]{2,1,0:T(8,128)(2,1)S(1)}, bf16[96,64,256]{2,1,0:T(8,128)(2,1)}, u32[]{:S(2)}) copy-start(bf16[96,64,256]{2,1,0:T(8,128)(2,1)} %kcache_ref.1) | copy-start | bytes 9437188
  2.7 0.8 %copy-start.1 = (bf16[4,4,2048]{2,1,0:T(4,128)(2,1)S(1)}, bf16[4,4,2048]{2,1,0:T(4,128)(2,1)}, u32[]{:S(2)}) copy-start(bf16[4,4,2048]{2,1,0:T(4,128)(2,1)} %queries_ref.1) | copy-start | bytes 196612
  3.5 0.8 %copy-start.2 = (f32[64,64]{1,0:T(8,128)S(1)}, f32[64,64]{1,0:T(8,128)}, u32[]{:S(2)}) copy-start(f32[64,64]{1,0:T(8,128)} %pre_ref.1) | copy-start | bytes 49156
  4.3 0.8 %copy-start.3 = (f32[64,64]{1,0:T(8,128)S(1)}, f32[64,64]{1,0:T(8,128)}, u32[]{:S(2)}) copy-start(f32[64,64]{1,0:T(8,128)} %post_ref.1) | copy-start | bytes 49156
  5.0 0.7 %copy-start.4 = (bf16[4,4,256]{2,1,0:T(4,128)(2,1)S(1)}, bf16[4,4,256]{2,1,0:T(4,128)(2,1)}, u32[]{:S(2)}) copy-start(bf16[4,4,256]{2,1,0:T(4,128)(2,1)} %newk_ref.1) | copy-start | bytes 24580
  5.7 0.7 %copy-start.5 = (bf16[4,4,256]{2,1,0:T(4,128)(2,1)S(1)}, bf16[4,4,256]{2,1,0:T(4,128)(2,1)}, u32[]{:S(2)}) copy-start(bf16[4,4,256]{2,1,0:T(4,128)(2,1)} %newv_ref.1) | copy-start | bytes 24580
  6.4 0.7 %copy-start.6 = (s32[4,16]{1,0:T(4,128)S(1)}, s32[4,16]{1,0:T(4,128)}, u32[]{:S(2)}) copy-start(s32[4,16]{1,0:T(4,128)} %tables_ref.1) | copy-start | bytes 772
  7.1 0.7 %copy-start.7 = (s32[4]{0:T(128)S(1)}, s32[4]{0:T(128)}, u32[]{:S(2)}) copy-start(s32[4]{0:T(128)} %lengths_ref.1) | copy-start | bytes 52

commit v2 on v1

--- a/solution.py
+++ b/solution.py
@@ -28,24 +28,32 @@
 def kernel(
     n_dp,
     n_tp,
+    send_hbm,
+    tables_hbm,
+    lengths_hbm,
+    kcache_ref,
+    vcache_ref,
+    queries_hbm,
+    newk_hbm,
+    newv_hbm,
+    pre_hbm,
+    post_hbm,
+    out_ref,
     send_ref,
     tables_ref,
     lengths_ref,
-    kcache_ref,
-    vcache_ref,
     queries_ref,
     newk_ref,
     newv_ref,
     pre_ref,
     post_ref,
-    out_ref,
     ext_k,
     ext_v,
     stage_k,
     stage_v,
     in_k,
     in_v,
-    q_wide,
+    q_rows,
     key_rows,
     value_rows,
     raw_send,
@@ -55,6 +63,7 @@
     blend_in,
     res,
     load_sem,
+    small_sem,
     ks_sem,
     kr_sem,
     vs_sem,
@@ -65,7 +74,7 @@
     br_sem,
 ):
     pages, page_len, width = kcache_ref.shape
-    cap = send_ref.shape[2]
+    cap = send_ref.shape[0]
     slots, maxp = tables_ref.shape
     steps = queries_ref.shape[1]
     heads = queries_ref.shape[2] // HEAD
@@ -92,108 +101,149 @@
         rows = pl.ds(part * chunk, chunk)
         return pltpu.make_async_copy(cache.at[rows], ext.at[rows], load_sem.at[which, part])
 
+    small = [
+        pltpu.make_async_copy(source, target, small_sem.at[i])
+        for i, (source, target) in enumerate(
+            (
+                (send_hbm, send_ref),
+                (tables_hbm, tables_ref),
+                (lengths_hbm, lengths_ref),
+                (queries_hbm, queries_ref),
+                (newk_hbm, newk_ref),
+                (newv_hbm, newv_ref),
+                (pre_hbm, pre_ref),
+                (post_hbm, post_ref),
+            )
+        )
+    ]
+    small[0].start()
     for part in range(parts):
         load(0, kcache_ref, ext_k, part).start()
+    for copy in small[1:]:
+        copy.start()
     for part in range(parts):
         load(1, vcache_ref, ext_v, part).start()
 
-    def page_copy(stage, inbox, s_sem, r_sem, o):
+    def target_of(o):
+        return lax.rem(dp + o + 1, n_dp)
+
+    def key_copy(g, o):
         return pltpu.make_async_remote_copy(
-            src_ref=stage.at[pl.ds(o * cap, cap)],
-            dst_ref=inbox.at[pl.ds(dp * cap, cap)],
-            send_sem=s_sem.at[o],
-            recv_sem=r_sem.at[o],
-            device_id={"dp": lax.rem(dp + o + 1, n_dp)},
+            src_ref=stage_k.at[g, pl.ds(o * cap, cap)],
+            dst_ref=in_k.at[g, pl.ds(dp * cap, cap)],
+            send_sem=ks_sem.at[g, o],
+            recv_sem=kr_sem.at[g, o],
+            device_id={"dp": target_of(o)},
             device_id_type=MESH,
         )
 
-    def stage_pages(stage, ext, o):
-        target = lax.rem(dp + o + 1, n_dp)
-        for c in range(cap):
-            page = jnp.maximum(send_ref[0, target, c], 0)
-            stage[o * cap + c] = ext[page]
-
+    def value_copy(o):
+        return pltpu.make_async_remote_copy(
+            src_ref=stage_v.at[pl.ds(o * cap, cap)],
+            dst_ref=in_v.at[pl.ds(dp * cap, cap)],
+            send_sem=vs_sem.at[o],
+            recv_sem=vr_sem.at[o],
+            device_id={"dp": target_of(o)},
+            device_id_type=MESH,
+        )
+
+    def listed(o, c):
+        return jnp.maximum(send_ref[c, 0, target_of(o)], 0)
+
+    def columns(g):
+        return slice(g * HEAD, (g + 1) * HEAD)
+
+    small[0].wait()
     pl.semaphore_wait(barrier, n_dp + n_tp - 2)
     for part in range(parts):
         load(0, kcache_ref, ext_k, part).wait()
 
-    def send_k(o):
-        stage_pages(stage_k, ext_k, o)
-        page_copy(stage_k, in_k, ks_sem, kr_sem, o).start()
-
-    each(n_dp - 1, send_k)
-
-    q_wide[...] = jnp.zeros_like(q_wide)
+    for g in range(groups):
+
+        def send_k(o):
+            for c in range(cap):
+                stage_k[g, o * cap + c] = ext_k[listed(o, c), :, columns(g)]
+            key_copy(g, o).start()
+
+        each(n_dp - 1, send_k)
+
+    for copy in small[1:]:
+        copy.wait()
+
     for s in range(slots):
         for h in range(heads):
-            g = h // group_size
-            q_wide[s, g, pl.ds(h, steps, stride=heads), :] = queries_ref[
-                s, :, h * HEAD : (h + 1) * HEAD
+            g, r = h // group_size, h % group_size
+            q_rows[s, g, pl.ds(r, steps, stride=group_size), :] = queries_ref[
+                s, :, columns(h)
             ].astype(jnp.float32)
     mix_t[0] = pre_ref[...].T
     mix_t[1] = post_ref[...].T
 
     for part in range(parts):
         load(1, vcache_ref, ext_v, part).wait()
-    each(n_dp - 1, lambda o: stage_pages(stage_v, ext_v, o))
-
-    def take_in(inbox, ext, copy):
-        def body(o):
-            copy(o).wait_recv()
-            source = lax.rem(dp + n_dp - 1 - o, n_dp)
-            for c in range(cap):
-                ext[pages + source * cap + c] = inbox[source * cap + c]
-
-        each(n_dp - 1, body)
-
-    take_in(in_k, ext_k, lambda o: page_copy(stage_k, in_k, ks_sem, kr_sem, o))
-    each(n_dp - 1, lambda o: page_copy(stage_v, in_v, vs_sem, vr_sem, o).start())
-
-    position = lax.broadcasted_iota(jnp.int32, (steps * heads, span), 1)
-
-    def raw_of(s):
+
+    def stage_values(o):
+        for c in range(cap):
+            stage_v[o * cap + c] = ext_v[listed(o, c)]
+
+    each(n_dp - 1, stage_values)
+
+    position = lax.broadcasted_iota(jnp.int32, (steps * group_size, span), 1)
+
+    def raw_of(g, s):
         for p in range(maxp):
-            key_rows[pl.ds(p * page_len, page_len), :] = ext_k[tables_ref[s, p]]
-        rows = jnp.concatenate([q_wide[s, g] for g in range(groups)], axis=1).astype(
-            jnp.bfloat16
-        )
+            key_rows[pl.ds(p * page_len, page_len), :] = ext_k[
+                tables_ref[s, p], :, columns(g)
+            ]
+        rows = q_rows[s, g].astype(jnp.bfloat16)
         contract = (((1,), (1,)), ((), ()))
         raw = lax.dot_general(
             rows, key_rows[...], contract, preferred_element_type=jnp.float32
         )
         fresh = lax.dot_general(
-            rows, newk_ref[s], contract, preferred_element_type=jnp.float32
+            rows, newk_ref[s, :, columns(g)], contract, preferred_element_type=jnp.float32
         )
         first = lengths_ref[s]
         for t in range(steps):
             raw = jnp.where(position == first + t, fresh[:, t : t + 1], raw)
-        return raw * (HEAD ** (-0.5))
-
-    def raw_copy(o, t):
+        return (raw * (HEAD ** (-0.5))).reshape(steps, group_size, span)
+
+    def raw_copy(g, o, first, count):
+        which = pl.ds(first, count)
         return pltpu.make_async_remote_copy(
-            src_ref=raw_send.at[o - 1, t],
-            dst_ref=raw_all.at[t, pl.ds(tp * heads, heads)],
-            send_sem=rs_sem.at[o - 1, t],
-            recv_sem=rr_sem.at[o - 1, t],
+            src_ref=raw_send.at[o - 1, g, which],
+            dst_ref=raw_all.at[which, pl.ds(tp * heads + g * group_size, group_size)],
+            send_sem=rs_sem.at[o - 1, g, first],
+            recv_sem=rr_sem.at[o - 1, g, first],
             device_id={"tp": lax.rem(tp + o, n_tp)},
             device_id_type=MESH,
         )
 
     half = n_tp // 2
     order = [half] + [o for o in range(1, n_tp) if o != half]
-    early = steps // 2
-    for o in order:
-        raw = raw_of(lax.rem(tp + o, n_tp))
-        for t in range(steps):
-            raw_send[o - 1, t] = raw[t * heads : (t + 1) * heads]
-        for t in range(early):
-            raw_copy(o, t).start()
-    for t in range(early, steps):
+    last = groups - 1
+    for g in range(groups):
+
+        def take_in(o):
+            key_copy(g, o).wait_recv()
+            source = lax.rem(dp + n_dp - 1 - o, n_dp)
+            for c in range(cap):
+                ext_k[pages + source * cap + c, :, columns(g)] = in_k[g, source * cap + c]
+
+        each(n_dp - 1, take_in)
+        if g == last:
+            each(n_dp - 1, lambda o: value_copy(o).start())
         for o in order:
-            raw_copy(o, t).start()
-    raw = raw_of(tp)
-    for t in range(steps):
-        raw_all[t, pl.ds(tp * heads, heads), :] = raw[t * heads : (t + 1) * heads]
+            raw_send[o - 1, g] = raw_of(g, lax.rem(tp + o, n_tp))
+            if g < last:
+                raw_copy(g, o, 0, steps).start()
+            else:
+                raw_copy(g, o, 0, 1).start()
+        if g == last:
+            for t in range(1, steps):
+                for o in order:
+                    raw_copy(g, o, t, 1).start()
+        raw_all[:, pl.ds(tp * heads + g * group_size, group_size), :] = raw_of(g, tp)
 
     def blend_copy(o, t):
         peer = lax.rem(tp + o, n_tp)
@@ -211,7 +261,10 @@
 
     def mix(t):
         for o in order:
-            raw_copy(o, t).wait_recv()
+            if t == 0:
+                for g in range(last):
+                    raw_copy(g, o, 0, steps).wait_recv()
+            raw_copy(last, o, t, 1).wait_recv()
         mixed = jnp.dot(
             mix_t[0], raw_all[t], precision=HIGHEST, preferred_element_type=jnp.float32
         )
@@ -239,7 +292,14 @@
 
     for t in range(steps - 1):
         mix(t)
-    take_in(in_v, ext_v, lambda o: page_copy(stage_v, in_v, vs_sem, vr_sem, o))
+
+    def take_in_values(o):
+        value_copy(o).wait_recv()
+        source = lax.rem(dp + n_dp - 1 - o, n_dp)
+        for c in range(cap):
+            ext_v[pages + source * cap + c] = in_v[source * cap + c]
+
+    each(n_dp - 1, take_in_values)
     for s in range(slots):
         gather_values(s)
     mix(steps - 1)
@@ -258,13 +318,16 @@
             ].astype(out_ref.dtype)
 
     def all_sent(o):
-        page_copy(stage_k, in_k, ks_sem, kr_sem, o).wait_send()
-        page_copy(stage_v, in_v, vs_sem, vr_sem, o).wait_send()
+        for g in range(groups):
+            key_copy(g, o).wait_send()
+        value_copy(o).wait_send()
 
     each(n_dp - 1, all_sent)
-    for t in range(steps):
-        for o in order:
-            raw_copy(o, t).wait_send()
+    for o in order:
+        for g in range(last):
+            raw_copy(g, o, 0, steps).wait_send()
+        for t in range(steps):
+            raw_copy(last, o, t, 1).wait_send()
             blend_copy(o, t).wait_send()
 
 
@@ -283,7 +346,8 @@
     post_mix,
 ):
     pages, page_len, width = kcache.shape
-    cap = send_pages.shape[2]
+    send_pages = jnp.transpose(send_pages, (2, 0, 1))
+    cap = send_pages.shape[0]
     slots, maxp = tables.shape
     steps = queries.shape[1]
     heads = queries.shape[2] // HEAD
@@ -292,44 +356,52 @@
     all_heads = heads * n_tp
     load_parts = 4
     vmem = pl.BlockSpec(memory_space=pltpu.VMEM)
-    smem = pl.BlockSpec(memory_space=pltpu.SMEM)
-    hbm = pl.BlockSpec(memory_space=pl.ANY)
+    hbm = pl.BlockSpec(memory_space=pltpu.HBM)
     moved = (n_dp - 1) * cap
     bf16, f32 = jnp.bfloat16, jnp.float32
     dma = pltpu.SemaphoreType.DMA
     return pl.pallas_call(
         functools.partial(kernel, n_dp, n_tp),
         out_shape=jax.ShapeDtypeStruct(queries.shape, bf16),
-        in_specs=[smem, smem, smem, hbm, hbm, vmem, vmem, vmem, vmem, vmem],
+        in_specs=[hbm] * 10,
         out_specs=vmem,
         scratch_shapes=[
+            pltpu.SMEM(send_pages.shape, jnp.int32),
+            pltpu.SMEM(tables.shape, jnp.int32),
+            pltpu.SMEM(lengths.shape, jnp.int32),
+            pltpu.VMEM(queries.shape, bf16),
+            pltpu.VMEM(new_keys.shape, bf16),
+            pltpu.VMEM(new_values.shape, bf16),
+            pltpu.VMEM(pre_mix.shape, f32),
+            pltpu.VMEM(post_mix.shape, f32),
             pltpu.VMEM((pages + n_dp * cap, page_len, width), bf16),
             pltpu.VMEM((pages + n_dp * cap, page_len, width), bf16),
+            pltpu.VMEM((groups, moved, page_len, HEAD), bf16),
             pltpu.VMEM((moved, page_len, width), bf16),
-            pltpu.VMEM((moved, page_len, width), bf16),
+            pltpu.VMEM((groups, n_dp * cap, page_len, HEAD), bf16),
             pltpu.VMEM((n_dp * cap, page_len, width), bf16),
-            pltpu.VMEM((n_dp * cap, page_len, width), bf16),
-            pltpu.VMEM((slots, groups, steps * heads, HEAD), f32),
-            pltpu.VMEM((span, width), bf16),
+            pltpu.VMEM((slots, groups, steps * heads // groups, HEAD), f32),
+            pltpu.VMEM((span, HEAD), bf16),
             pltpu.VMEM((slots, span, width), bf16),
-            pltpu.VMEM((n_tp - 1, steps, heads, span), f32),
+            pltpu.VMEM((n_tp - 1, groups, steps, heads // groups, span), f32),
             pltpu.VMEM((steps, all_heads, span), f32),
             pltpu.VMEM((2, all_heads, all_heads), f32),
             pltpu.VMEM((steps, all_heads, span), bf16),
             pltpu.VMEM((slots, steps * heads, span), bf16),
             pltpu.VMEM((groups, steps * heads, HEAD), f32),
             dma((2, load_parts)),
+            dma((8,)),
+            dma((groups, n_dp - 1)),
+            dma((groups, n_dp - 1)),
             dma((n_dp - 1,)),
             dma((n_dp - 1,)),
-            dma((n_dp - 1,)),
-            dma((n_dp - 1,)),
-            dma((n_tp - 1, steps)),
-            dma((n_tp - 1, steps)),
+            dma((n_tp - 1, groups, steps)),
+            dma((n_tp - 1, groups, steps)),
             dma((n_tp - 1, steps)),
             dma((n_tp - 1, steps)),
         ],
         compiler_params=pltpu.CompilerParams(
-            collective_id=0, has_side_effects=True, vmem_limit_bytes=48 * 1024 * 1024
+            collective_id=0, has_side_effects=True, vmem_limit_bytes=64 * 1024 * 1024
         ),
     )(
         send_pages,

time: 42.2 us -> 32.5 us (0.77)
  local copies, waits for them, and re-layouts: 8.37 us -> 1.49 us
  Pallas kernels: 33.3 us -> 30.8 us
    unnamed x18 -> x1, local copies, waits for them, and re-layouts: 8.37 us -> 1.49 us
    pallas_call x1, Pallas kernels: 33.3 us -> 30.8 us  [on_device(): pl.pallas_call(functools.partial(kernel, n_dp, n_tp), out_shape=jax.Shape...]
where the time goes in v2:
time: 32.5 us; the launch traced here: 32.3 us
  Pallas kernels  30.8 us (95%)
  local copies, waits for them, and re-layouts  1.49 us (5%)
    pallas_call x1, Pallas kernels, on_device(): pl.pallas_call(functools.partial(kernel, n_dp, n_tp), out_shape=jax.Shape...  30.8 us
    unnamed x1, local copies, waits for them, and re-layouts  1.49 us

profile of v2, /device:TPU:0, one launch (start us, length us, event | category | flops | bytes accessed | tf_op | source)
XLA Modules:
  0.0 32.3 jit_solution(6825166900370503429)
XLA Ops:
  0.0 30.8 %shard_map.100 = bf16[4,4,2048]{2,1,0:T(4,128)(2,1)} custom-call(s32[3,1,4]{2,1,0:T(1,128)} %bitcast.1, s32[4,16]{1,0:T(4,128)} %tables_hbm.1, s32[4]{0:T(128)} %lengths_hbm.1, bf16[96,64,256]{2,1,0:T(8,128)(2,1)} %kcache_ref.1, bf16[96,64,256]{2,1,0:T(8,128)(2,1)} %vcache_ref.1, bf16[4,4,2048]{2,1,0:T(4,128)(2,1)} %queries_hbm.1, ...), custom_call_target="tpu_custom_call" | custom-call | tf_op jit(solution)/shard_map/pallas_call | solution.py:363
  30.9 1.5 %copy.12 = bf16[4,4,2048]{2,1,0:T(4,128)(2,1)} copy(bf16[4,4,2048]{2,1,0:T(4,128)(2,1)} %shard_map.100) | data formatting | bytes 131072

commit v3 on v2

--- a/solution.py
+++ b/solution.py
@@ -290,8 +290,6 @@
                 page = jnp.where(row == first + t - p * page_len, fresh[t : t + 1, :], page)
             value_rows[s, pl.ds(p * page_len, page_len), :] = page.astype(jnp.bfloat16)
 
-    for t in range(steps - 1):
-        mix(t)
 
     def take_in_values(o):
         value_copy(o).wait_recv()
@@ -302,7 +300,8 @@
     each(n_dp - 1, take_in_values)
     for s in range(slots):
         gather_values(s)
-    mix(steps - 1)
+    for t in range(steps):
+        mix(t)
 
     for o in [0] + [n_tp - o for o in order]:
         s = lax.rem(tp + o, n_tp)

time: 32.5 us -> 34.9 us (1.074)
  Pallas kernels: 30.8 us -> 33.2 us
    pallas_call x1, Pallas kernels: 30.8 us -> 33.2 us  [on_device(): pl.pallas_call(functools.partial(kernel, n_dp, n_tp), out_shape=jax.Shape...]
where the time goes in v3:
time: 34.9 us; the launch traced here: 34.7 us
  Pallas kernels  33.2 us (95%)
  local copies, waits for them, and re-layouts  1.49 us (4%)
    pallas_call x1, Pallas kernels, on_device(): pl.pallas_call(functools.partial(kernel, n_dp, n_tp), out_shape=jax.Shape...  33.2 us
    unnamed x1, local copies, waits for them, and re-layouts  1.49 us

profile of v3, /device:TPU:0, one launch (start us, length us, event | category | flops | bytes accessed | tf_op | source)
XLA Modules:
  0.0 34.7 jit_solution(8160314383188342793)
XLA Ops:
  0.0 33.2 %shard_map.100 = bf16[4,4,2048]{2,1,0:T(4,128)(2,1)} custom-call(s32[3,1,4]{2,1,0:T(1,128)} %bitcast.1, s32[4,16]{1,0:T(4,128)} %tables_hbm.1, s32[4]{0:T(128)} %lengths_hbm.1, bf16[96,64,256]{2,1,0:T(8,128)(2,1)} %kcache_ref.1, bf16[96,64,256]{2,1,0:T(8,128)(2,1)} %vcache_ref.1, bf16[4,4,2048]{2,1,0:T(4,128)(2,1)} %queries_hbm.1, ...), custom_call_target="tpu_custom_call" | custom-call | tf_op jit(solution)/shard_map/pallas_call | solution.py:362
  33.2 1.5 %copy.12 = bf16[4,4,2048]{2,1,0:T(4,128)(2,1)} copy(bf16[4,4,2048]{2,1,0:T(4,128)(2,1)} %shard_map.100) | data formatting | bytes 131072
